TPU v7x, 32 devices: a whole 2x2x4 slice. The times are simulated.
32 devices in a mesh: ctx: 8 (over z, x), head: 4 (over y, core).
Axes of the slice: x: 2, y: 2, z: 4, core: 2. Of those that a mesh axis runs over, the one named last changes fastest.
Arguments:
- query_states: bfloat16 [4096, 3584], P('ctx', 'head'), may hold values from -15 to 15
- key_states: bfloat16 [4096, 512], P('ctx', 'head'), may hold values from -6 to 6
- value_states: bfloat16 [4096, 512], P('ctx', 'head'), may hold values from -6 to 6
- out_weight: bfloat16 [3584, 3584], P('head'), may hold values from -0.29882812 to 0.29882812
- block_order: int32 [16], replicated, may hold values from 0 to 15, each once
- page_owner: int32 [256, 1], replicated, may hold values from 0 to 7; in each aligned block of 32 rows (0 to 31, 32 to 63, ...) at most 8 rows name the same one
- held_pages: int32 [8], replicated, may hold values from 0 to 64
Outputs:
- layer_output: bfloat16 [4096, 3584], P(('ctx', 'head'))
- page_values: bfloat16 [1024, 16, 1024], P('ctx', None, 'head')
- page_scales: float32 [8, 16384], P('head', 'ctx')
Inputs may be any that keep to these rules, and one draw needn't show every extreme that they name: `block_order`: each number once. `page_owner`: among the pages of one device (aligned blocks of 32 rows) no owner is named more than 8 times.
All inputs are finite; a program needn't handle non-finite values. Where the computation divides by a largest or mean magnitude, that divisor is 1e-20 or more.
Results may differ from a plain program's by a relative error of at most 0.012.
Values may be sent and summed in bfloat16 or wider, within the bound.
A program may use at most 64 MiB of HBM per device.

v0:
```python
import math

import jax
import jax.numpy as jnp
from jax import lax
from jax.sharding import PartitionSpec as P

HD = 128
PAGE = 16
BLOCK = 256


NEG_FILL = -1e30


def positions(first_row, piece_len, block_order):
    rows_at = first_row + jnp.arange(piece_len, dtype=jnp.int32)
    block_ids = jnp.arange(block_order.shape[0], dtype=jnp.int32)
    matches = (rows_at // BLOCK)[:, None] == block_ids[None, :]
    starts = jnp.sum(jnp.where(matches, block_order[None, :], 0), axis=1)
    return starts * BLOCK + rows_at % BLOCK


def tile_update(soft_state, key_tile, value_tile, key_pos, query_heads, query_pos):
    top_score, norm_sum, weighted = soft_state
    scores = jnp.einsum(
        "qhgd,khd->hgqk", query_heads, key_tile, preferred_element_type=jnp.float32
    ) * (1.0 / math.sqrt(HD))
    allowed = (key_pos[None, :] <= query_pos[:, None])[None, None]
    new_top = jnp.maximum(top_score, jnp.max(jnp.where(allowed, scores, NEG_FILL), axis=-1))
    weights = jnp.where(allowed, jnp.exp(scores - new_top[..., None]), 0.0)
    factor = jnp.exp(top_score - new_top)
    norm_sum = norm_sum * factor + jnp.sum(weights, axis=-1)
    contrib = jnp.einsum(
        "hgqk,khd->qhgd",
        weights.astype(jnp.bfloat16),
        value_tile,
        preferred_element_type=jnp.float32,
    )
    weighted = weighted * jnp.transpose(factor, (2, 0, 1))[..., None] + contrib
    return (new_top, norm_sum, weighted)


def attend_piece(soft_state, key_piece, value_piece, query_heads, query_pos, block_order):
    piece_len = key_piece.shape[0]
    kv_local = key_piece.shape[1] // HD
    sub_len = math.gcd(piece_len, 512)
    tile_total = piece_len // sub_len
    key_blocks = key_piece.reshape(tile_total, sub_len, kv_local, HD)
    value_blocks = value_piece.reshape(tile_total, sub_len, kv_local, HD)
    last_query = jnp.max(query_pos)

    def one_tile(carried, inputs):
        key_tile, value_tile, tile_index = inputs
        key_pos = positions(tile_index * sub_len, sub_len, block_order)
        carried = lax.cond(
            jnp.min(key_pos) <= last_query,
            lambda unchanged: tile_update(
                unchanged, key_tile, value_tile, key_pos, query_heads, query_pos
            ),
            lambda unchanged: unchanged,
            carried,
        )
        return (carried, None)

    soft_state, _ = lax.scan(
        one_tile, soft_state, (key_blocks, value_blocks, jnp.arange(tile_total, dtype=jnp.int32))
    )
    return soft_state


def shards(query_states, key_states, value_states, out_weight, block_order, page_owner, held_pages):
    tok_rows = query_states.shape[0]
    col_count = query_states.shape[1]
    kv_local = key_states.shape[1] // HD
    group_size = query_states.shape[1] // key_states.shape[1]
    row_width = 2 * kv_local * HD
    ctx_index = lax.axis_index("ctx")
    ctx_count = lax.axis_size("ctx")
    pages_dev = tok_rows // PAGE
    per_peer = max(2, 2 * pages_dev // ctx_count)
    slot_count = 2 * ctx_count * per_peer
    work_pos = positions(ctx_index * tok_rows, tok_rows, block_order)
    query_heads = query_states.reshape(tok_rows, kv_local, group_size, HD)
    start_state = (
        jnp.full((kv_local, group_size, tok_rows), NEG_FILL, jnp.float32),
        jnp.zeros((kv_local, group_size, tok_rows), jnp.float32),
        jnp.zeros((tok_rows, kv_local, group_size, HD), jnp.float32),
    )
    owners = page_owner[:, 0]
    held_here = lax.dynamic_index_in_dim(held_pages, ctx_index, 0, keepdims=False)
    folded = attend_piece(
        start_state,
        lax.all_gather(key_states, "ctx", axis=0, tiled=True),
        lax.all_gather(value_states, "ctx", axis=0, tiled=True),
        query_heads,
        work_pos,
        block_order,
    )
    both_local = jnp.stack(
        [key_states.reshape(tok_rows, kv_local, HD), value_states.reshape(tok_rows, kv_local, HD)],
        axis=2,
    ).reshape(pages_dev, PAGE, row_width)
    local_owner = lax.dynamic_slice_in_dim(owners, ctx_index * pages_dev, pages_dev)
    owner_hot = (local_owner[:, None] == jnp.arange(ctx_count, dtype=jnp.int32)[None, :]).astype(
        jnp.int32
    )
    local_rank = jnp.sum((jnp.cumsum(owner_hot, axis=0) - 1) * owner_hot, axis=1)
    send_rows = local_owner * per_peer + local_rank
    outgoing = (
        jnp.zeros((ctx_count * per_peer, PAGE, row_width), jnp.bfloat16)
        .at[send_rows]
        .set(both_local)
    )
    incoming = lax.all_to_all(outgoing, "ctx", split_axis=0, concat_axis=0, tiled=True)
    owned_grid = (owners.reshape(ctx_count, pages_dev) == ctx_index).astype(jnp.int32)
    within = jnp.cumsum(owned_grid, axis=1) - 1
    rank_global = (jnp.cumsum(owned_grid.reshape(-1)) - 1).reshape(ctx_count, pages_dev)
    sources = jnp.arange(ctx_count, dtype=jnp.int32)[:, None]
    buffer_row = jnp.where(owned_grid == 1, sources * per_peer + within, ctx_count * per_peer)
    target = jnp.where(owned_grid == 1, held_here + rank_global, slot_count)
    store_slot = (
        jnp.full((ctx_count * per_peer + 1,), slot_count, jnp.int32)
        .at[buffer_row.reshape(-1)]
        .set(target.reshape(-1))[: ctx_count * per_peer]
    )
    page_store = (
        jnp.zeros((slot_count + 1, PAGE, row_width), jnp.bfloat16)
        .at[store_slot]
        .set(incoming)[:slot_count]
    )
    top_score, norm_sum, weighted = folded
    attended = (
        (weighted / jnp.transpose(norm_sum, (2, 0, 1))[..., None])
        .reshape(tok_rows, col_count)
        .astype(jnp.bfloat16)
    )
    layer_output = lax.psum_scatter(
        jnp.dot(attended, out_weight, preferred_element_type=jnp.float32).astype(jnp.bfloat16),
        "head",
        scatter_dimension=0,
        tiled=True,
    )
    split_store = page_store.astype(jnp.float32).reshape(slot_count, PAGE, 2 * kv_local, HD)
    page_scale = jnp.max(jnp.abs(split_store), axis=-1) + 1e-06
    page_values = (
        (split_store / page_scale[..., None])
        .astype(jnp.bfloat16)
        .reshape(slot_count, PAGE, row_width)
    )
    page_scales = jnp.transpose(page_scale.reshape(slot_count * PAGE, 2 * kv_local))
    return (layer_output, page_values, page_scales)


def solution(mesh):
    in_specs = (
        P("ctx", "head"),
        P("ctx", "head"),
        P("ctx", "head"),
        P("head", None),
        P(),
        P(),
        P(),
    )
    out_specs = (P(("ctx", "head"), None), P("ctx", None, "head"), P("head", "ctx"))
    return jax.shard_map(shards, mesh=mesh, in_specs=in_specs, out_specs=out_specs, check_vma=False)
```

profile of v0, /device:TPU:0, one launch (start us, length us, event | category | flops | bytes accessed | tf_op | source)
XLA Modules:
  0.0 237.5 jit_solution(3978989290634156976)
XLA Ops:
  11.6 41.5 %all-gather.5.cloned.1.call-done = bf16[4096,128]{1,0:T(8,128)(2,1)} async-done(((bf16[512,128]{1,0:T(8,128)(2,1)}), bf16[4096,128]{1,0:T(8,128)(2,1)}) %all-gather.5.cloned.1.call-update) | async-done | bytes 1048592 | tf_op jit(solution)/shard_map/all_gather | solution.py:95
  53.0 2.3 copy.33
  55.3 38.8 %all-gather.3.cloned.1.call-done = bf16[4096,128]{1,0:T(8,128)(2,1)} async-done(((bf16[512,128]{1,0:T(8,128)(2,1)}), bf16[4096,128]{1,0:T(8,128)(2,1)}) %all-gather.3.cloned.1.call-update) | async-done | bytes 1048592 | tf_op jit(solution)/shard_map/all_gather | solution.py:94
  94.3 81.9 %while.16 = (s32[]{:T(128)}, f32[1,7,512]{2,1,0:T(8,128)S(1)}, f32[1,7,512]{2,1,0:T(8,128)S(1)}, f32[512,1,7,128]{0,3,2,1:T(8,128)S(1)}, s32[8]{0:T(128)S(1)}, /...) while((s32[]{:T(128)}, f32[1,7,512]{2,1,0:T(8,128)S(1)}, ...), condition=%wide.region_9.10_spmd, body=%wide.region_2.9_spmd.sunk | while | flops 960939520 | bytes 28163448 | solution.py:66
  97.6 7.0 %conditional.2 = ((f32[1,7,512]{2,1,0:T(8,128)S(1)}, f32[1,7,512]{2,1,0:T(8,128)S(1)}, f32[512,1,7,128]{0,3,2,1:T(8,128)S(1)})) conditional(s32[]{:T(128)} %convert_element_type.78, (f32[1,7,512]{2,1,0:T(8,128)S(1)}, f32[1,7,512]{2,1,0:T(8,128)S(1)}, f32[512,1,7,128]{0,3,2,1:T(8,128)S(1)}) %tuple.56, (s32[512]{0:T(512)S(1)}, s32[512]{0:T(512)S(1)}, ...), branch_computations={%region_5.5_spmd, %region_6.8_spmd} | conditional | flops 960899584 | bytes 28152864 | solution.py:56
  97.8 2.2 fusion
  100.1 1.5 fusion.4
  101.6 2.9 %bitcast_add_fusion = f32[512,1,7,128]{0,3,2,1:T(8,128)S(1)} fusion(f32[512,1,7,128]{0,3,2,1:T(8,128)S(1)} %get-tuple-element.211, f32[512,512,7]{1,0,2:T(8,128)S(1)} %get-tuple-element.310, f32[7,512]{1,0:T(8,128)S(1)} %bitcast.90, pred[512,512]{0,1:T(8,128)(4,1)S(1)} %broadcast_compare_fusion, f32[512,7]{0,1:T(8,128)S(1)} %get-tuple-element.301, ...), kind=kOutput, calls=%fused_computation.13 | convolution fusion | flops 478019584 | bytes 11432448 | tf_op jit(solution)/shard_map/while/body/eval_jaxpr/cond/branch_1_fun/hgqk,khd->qhgd/dot_general | solution.py:34
  107.8 7.0 %conditional.2 = ((f32[1,7,512]{2,1,0:T(8,128)S(1)}, f32[1,7,512]{2,1,0:T(8,128)S(1)}, f32[512,1,7,128]{0,3,2,1:T(8,128)S(1)})) conditional(s32[]{:T(128)} %convert_element_type.78, (f32[1,7,512]{2,1,0:T(8,128)S(1)}, f32[1,7,512]{2,1,0:T(8,128)S(1)}, f32[512,1,7,128]{0,3,2,1:T(8,128)S(1)}) %tuple.56, (s32[512]{0:T(512)S(1)}, s32[512]{0:T(512)S(1)}, ...), branch_computations={%region_5.5_spmd, %region_6.8_spmd} | conditional | flops 960899584 | bytes 28152864 | solution.py:56
  108.0 2.2 fusion
  110.3 1.5 fusion.4
  111.8 2.9 %bitcast_add_fusion = f32[512,1,7,128]{0,3,2,1:T(8,128)S(1)} fusion(f32[512,1,7,128]{0,3,2,1:T(8,128)S(1)} %get-tuple-element.211, f32[512,512,7]{1,0,2:T(8,128)S(1)} %get-tuple-element.310, f32[7,512]{1,0:T(8,128)S(1)} %bitcast.90, pred[512,512]{0,1:T(8,128)(4,1)S(1)} %broadcast_compare_fusion, f32[512,7]{0,1:T(8,128)S(1)} %get-tuple-element.301, ...), kind=kOutput, calls=%fused_computation.13 | convolution fusion | flops 478019584 | bytes 11432448 | tf_op jit(solution)/shard_map/while/body/eval_jaxpr/cond/branch_1_fun/hgqk,khd->qhgd/dot_general | solution.py:34
  118.0 7.0 %conditional.2 = ((f32[1,7,512]{2,1,0:T(8,128)S(1)}, f32[1,7,512]{2,1,0:T(8,128)S(1)}, f32[512,1,7,128]{0,3,2,1:T(8,128)S(1)})) conditional(s32[]{:T(128)} %convert_element_type.78, (f32[1,7,512]{2,1,0:T(8,128)S(1)}, f32[1,7,512]{2,1,0:T(8,128)S(1)}, f32[512,1,7,128]{0,3,2,1:T(8,128)S(1)}) %tuple.56, (s32[512]{0:T(512)S(1)}, s32[512]{0:T(512)S(1)}, ...), branch_computations={%region_5.5_spmd, %region_6.8_spmd} | conditional | flops 960899584 | bytes 28152864 | solution.py:56
  118.3 2.2 fusion
  120.5 1.5 fusion.4
  122.1 2.9 %bitcast_add_fusion = f32[512,1,7,128]{0,3,2,1:T(8,128)S(1)} fusion(f32[512,1,7,128]{0,3,2,1:T(8,128)S(1)} %get-tuple-element.211, f32[512,512,7]{1,0,2:T(8,128)S(1)} %get-tuple-element.310, f32[7,512]{1,0:T(8,128)S(1)} %bitcast.90, pred[512,512]{0,1:T(8,128)(4,1)S(1)} %broadcast_compare_fusion, f32[512,7]{0,1:T(8,128)S(1)} %get-tuple-element.301, ...), kind=kOutput, calls=%fused_computation.13 | convolution fusion | flops 478019584 | bytes 11432448 | tf_op jit(solution)/shard_map/while/body/eval_jaxpr/cond/branch_1_fun/hgqk,khd->qhgd/dot_general | solution.py:34
  128.3 7.0 %conditional.2 = ((f32[1,7,512]{2,1,0:T(8,128)S(1)}, f32[1,7,512]{2,1,0:T(8,128)S(1)}, f32[512,1,7,128]{0,3,2,1:T(8,128)S(1)})) conditional(s32[]{:T(128)} %convert_element_type.78, (f32[1,7,512]{2,1,0:T(8,128)S(1)}, f32[1,7,512]{2,1,0:T(8,128)S(1)}, f32[512,1,7,128]{0,3,2,1:T(8,128)S(1)}) %tuple.56, (s32[512]{0:T(512)S(1)}, s32[512]{0:T(512)S(1)}, ...), branch_computations={%region_5.5_spmd, %region_6.8_spmd} | conditional | flops 960899584 | bytes 28152864 | solution.py:56
  128.5 2.2 fusion
  130.8 1.5 fusion.4
  132.3 2.9 %bitcast_add_fusion = f32[512,1,7,128]{0,3,2,1:T(8,128)S(1)} fusion(f32[512,1,7,128]{0,3,2,1:T(8,128)S(1)} %get-tuple-element.211, f32[512,512,7]{1,0,2:T(8,128)S(1)} %get-tuple-element.310, f32[7,512]{1,0:T(8,128)S(1)} %bitcast.90, pred[512,512]{0,1:T(8,128)(4,1)S(1)} %broadcast_compare_fusion, f32[512,7]{0,1:T(8,128)S(1)} %get-tuple-element.301, ...), kind=kOutput, calls=%fused_computation.13 | convolution fusion | flops 478019584 | bytes 11432448 | tf_op jit(solution)/shard_map/while/body/eval_jaxpr/cond/branch_1_fun/hgqk,khd->qhgd/dot_general | solution.py:34
  138.5 7.0 %conditional.2 = ((f32[1,7,512]{2,1,0:T(8,128)S(1)}, f32[1,7,512]{2,1,0:T(8,128)S(1)}, f32[512,1,7,128]{0,3,2,1:T(8,128)S(1)})) conditional(s32[]{:T(128)} %convert_element_type.78, (f32[1,7,512]{2,1,0:T(8,128)S(1)}, f32[1,7,512]{2,1,0:T(8,128)S(1)}, f32[512,1,7,128]{0,3,2,1:T(8,128)S(1)}) %tuple.56, (s32[512]{0:T(512)S(1)}, s32[512]{0:T(512)S(1)}, ...), branch_computations={%region_5.5_spmd, %region_6.8_spmd} | conditional | flops 960899584 | bytes 28152864 | solution.py:56
  138.7 2.2 fusion
  141.0 1.5 fusion.4
  142.6 2.9 %bitcast_add_fusion = f32[512,1,7,128]{0,3,2,1:T(8,128)S(1)} fusion(f32[512,1,7,128]{0,3,2,1:T(8,128)S(1)} %get-tuple-element.211, f32[512,512,7]{1,0,2:T(8,128)S(1)} %get-tuple-element.310, f32[7,512]{1,0:T(8,128)S(1)} %bitcast.90, pred[512,512]{0,1:T(8,128)(4,1)S(1)} %broadcast_compare_fusion, f32[512,7]{0,1:T(8,128)S(1)} %get-tuple-element.301, ...), kind=kOutput, calls=%fused_computation.13 | convolution fusion | flops 478019584 | bytes 11432448 | tf_op jit(solution)/shard_map/while/body/eval_jaxpr/cond/branch_1_fun/hgqk,khd->qhgd/dot_general | solution.py:34
  148.7 7.0 %conditional.2 = ((f32[1,7,512]{2,1,0:T(8,128)S(1)}, f32[1,7,512]{2,1,0:T(8,128)S(1)}, f32[512,1,7,128]{0,3,2,1:T(8,128)S(1)})) conditional(s32[]{:T(128)} %convert_element_type.78, (f32[1,7,512]{2,1,0:T(8,128)S(1)}, f32[1,7,512]{2,1,0:T(8,128)S(1)}, f32[512,1,7,128]{0,3,2,1:T(8,128)S(1)}) %tuple.56, (s32[512]{0:T(512)S(1)}, s32[512]{0:T(512)S(1)}, ...), branch_computations={%region_5.5_spmd, %region_6.8_spmd} | conditional | flops 960899584 | bytes 28152864 | solution.py:56
  149.0 2.2 fusion
  151.2 1.5 fusion.4
  152.8 2.9 %bitcast_add_fusion = f32[512,1,7,128]{0,3,2,1:T(8,128)S(1)} fusion(f32[512,1,7,128]{0,3,2,1:T(8,128)S(1)} %get-tuple-element.211, f32[512,512,7]{1,0,2:T(8,128)S(1)} %get-tuple-element.310, f32[7,512]{1,0:T(8,128)S(1)} %bitcast.90, pred[512,512]{0,1:T(8,128)(4,1)S(1)} %broadcast_compare_fusion, f32[512,7]{0,1:T(8,128)S(1)} %get-tuple-element.301, ...), kind=kOutput, calls=%fused_computation.13 | convolution fusion | flops 478019584 | bytes 11432448 | tf_op jit(solution)/shard_map/while/body/eval_jaxpr/cond/branch_1_fun/hgqk,khd->qhgd/dot_general | solution.py:34
  159.0 7.0 %conditional.2 = ((f32[1,7,512]{2,1,0:T(8,128)S(1)}, f32[1,7,512]{2,1,0:T(8,128)S(1)}, f32[512,1,7,128]{0,3,2,1:T(8,128)S(1)})) conditional(s32[]{:T(128)} %convert_element_type.78, (f32[1,7,512]{2,1,0:T(8,128)S(1)}, f32[1,7,512]{2,1,0:T(8,128)S(1)}, f32[512,1,7,128]{0,3,2,1:T(8,128)S(1)}) %tuple.56, (s32[512]{0:T(512)S(1)}, s32[512]{0:T(512)S(1)}, ...), branch_computations={%region_5.5_spmd, %region_6.8_spmd} | conditional | flops 960899584 | bytes 28152864 | solution.py:56
  159.2 2.2 fusion
  161.5 1.5 fusion.4
  163.0 2.9 %bitcast_add_fusion = f32[512,1,7,128]{0,3,2,1:T(8,128)S(1)} fusion(f32[512,1,7,128]{0,3,2,1:T(8,128)S(1)} %get-tuple-element.211, f32[512,512,7]{1,0,2:T(8,128)S(1)} %get-tuple-element.310, f32[7,512]{1,0:T(8,128)S(1)} %bitcast.90, pred[512,512]{0,1:T(8,128)(4,1)S(1)} %broadcast_compare_fusion, f32[512,7]{0,1:T(8,128)S(1)} %get-tuple-element.301, ...), kind=kOutput, calls=%fused_computation.13 | convolution fusion | flops 478019584 | bytes 11432448 | tf_op jit(solution)/shard_map/while/body/eval_jaxpr/cond/branch_1_fun/hgqk,khd->qhgd/dot_general | solution.py:34
  169.2 7.0 %conditional.2 = ((f32[1,7,512]{2,1,0:T(8,128)S(1)}, f32[1,7,512]{2,1,0:T(8,128)S(1)}, f32[512,1,7,128]{0,3,2,1:T(8,128)S(1)})) conditional(s32[]{:T(128)} %convert_element_type.78, (f32[1,7,512]{2,1,0:T(8,128)S(1)}, f32[1,7,512]{2,1,0:T(8,128)S(1)}, f32[512,1,7,128]{0,3,2,1:T(8,128)S(1)}) %tuple.56, (s32[512]{0:T(512)S(1)}, s32[512]{0:T(512)S(1)}, ...), branch_computations={%region_5.5_spmd, %region_6.8_spmd} | conditional | flops 960899584 | bytes 28152864 | solution.py:56
  169.4 2.2 fusion
  171.7 1.5 fusion.4
  173.3 2.9 %bitcast_add_fusion = f32[512,1,7,128]{0,3,2,1:T(8,128)S(1)} fusion(f32[512,1,7,128]{0,3,2,1:T(8,128)S(1)} %get-tuple-element.211, f32[512,512,7]{1,0,2:T(8,128)S(1)} %get-tuple-element.310, f32[7,512]{1,0:T(8,128)S(1)} %bitcast.90, pred[512,512]{0,1:T(8,128)(4,1)S(1)} %broadcast_compare_fusion, f32[512,7]{0,1:T(8,128)S(1)} %get-tuple-element.301, ...), kind=kOutput, calls=%fused_computation.13 | convolution fusion | flops 478019584 | bytes 11432448 | tf_op jit(solution)/shard_map/while/body/eval_jaxpr/cond/branch_1_fun/hgqk,khd->qhgd/dot_general | solution.py:34
  176.5 8.3 %convolution_convert_fusion = bf16[512,3584]{1,0:T(8,128)(2,1)} fusion(bf16[512,896]{0,1:T(8,128)(2,1)S(1)} %bitcast.93, bf16[896,3584]{1,0:T(8,128)(2,1)} %param.14), kind=kOutput, calls=%fused_computation.42 | convolution fusion | flops 3290169344 | bytes 11010048 | tf_op jit(solution)/shard_map/dot_general | solution.py:139
  187.3 3.9 %scatter_fusion = bf16[64,16,256]{2,1,0:T(8,128)(2,1)} fusion(bf16[64,16,256]{2,1,0:T(8,128)(2,1)} %broadcast_in_dim.106, s32[32]{0:T(128)S(1)} %fusion.32, bf16[32,16,256]{2,1,0:T(8,128)(2,1)S(1)} %reshape.248), kind=kCustom, calls=%fused_computation.1 | custom fusion | bytes 786560 | tf_op jit(solution)/shard_map/scatter | solution.py:113
  191.2 3.5 %all-to-all-start = ((bf16[64,16,256]{2,1,0:T(8,128)(2,1)}), bf16[64,16,256]{2,1,0:T(8,128)(2,1)S(1)}, u32[]{:S(2)}, u32[]{:S(2)}) async-start(bf16[64,16,256]{2,1,0:T(8,128)(2,1)} %scatter_fusion), calls=%async_computation.1 | async-start | bytes 1048576 | tf_op jit(solution)/shard_map/all_to_all | solution.py:115
  198.2 1.6 scatter_custom_fusion
  199.8 8.7 %all-to-all-done = bf16[64,16,256]{2,1,0:T(8,128)(2,1)S(1)} async-done(((bf16[64,16,256]{2,1,0:T(8,128)(2,1)}), bf16[64,16,256]{2,1,0:T(8,128)(2,1)S(1)}, u32[]{:S(2)}, u32[]{:S(2)}) %all-to-all-start) | async-done | bytes 524320 | tf_op jit(solution)/shard_map/all_to_all | solution.py:115
  208.6 2.5 %scatter_fusion.1 = bf16[129,16,256]{2,1,0:T(8,128)(2,1)S(1)} fusion(bf16[129,16,256]{2,1,0:T(8,128)(2,1)S(1)} %broadcast_in_dim.101, s32[64]{0:T(128)S(1)} %compare_select_fusion.2, bf16[64,16,256]{2,1,0:T(8,128)(2,1)S(1)} %all-to-all-done), kind=kCustom, calls=%fused_computation.2 | custom fusion | bytes 1573120 | tf_op jit(solution)/shard_map/scatter | solution.py:130
  211.1 1.7 convert_abs_fusion
  212.8 2.3 abs.7
  215.1 3.2 %reduce_max.30 = f32[128,16,2]{2,1,0:T(8,128)} reduce(f32[128,16,2,128]{3,2,1,0:T(2,128)S(1)} %abs.7, f32[]{:T(128)} %constant.176.clone.1), dimensions={3}, to_apply=%region_19.20 | reduce | flops 520192 | bytes 2113540 | tf_op jit(solution)/shard_map/reduce_max | solution.py:145
  219.6 3.5 %div.50 = f32[128,16,2,128]{3,2,1,0:T(2,128)} broadcast(f32[128,16,2]{2,1,0:T(8,128)S(1)} %broadcast_add_fusion), dimensions={0,1,2} | broadcast | bytes 2113536 | tf_op jit(solution)/shard_map/div | solution.py:147
  223.1 3.9 %div.51 = f32[128,16,256]{2,1,0:T(8,128)} reshape(f32[128,16,2,128]{3,2,1,0:T(2,128)} %div.50) | data formatting | bytes 4194304 | tf_op jit(solution)/shard_map/div | solution.py:147
  227.9 3.1 %fusion.26 = bf16[128,16,256]{2,1,0:T(8,128)(2,1)} fusion(f32[128,16,256]{2,1,0:T(8,128)} %div.51, bf16[129,16,256]{2,1,0:T(8,128)(2,1)S(1)} %scatter_fusion.1), kind=kLoop, calls=%fused_computation.45 | loop fusion | flops 1572864 | bytes 4194304 | tf_op jit(solution)/shard_map/convert_element_type | solution.py:148
  (119 shorter events, 25.9 us)
Async XLA Ops:
  7.2 3.7 %copy-start.2 = (s32[16]{0:T(128)S(1)}, s32[16]{0:T(128)}, u32[]{:S(2)}) copy-start(s32[16]{0:T(128)} %param.15) | copy-start | bytes 196
  7.2 45.8 %all-gather.5.cloned.1.call-start = ((), (), s32[]{:S(2)}) async-start(), calls=%async_computation.3 | async-start | bytes 1179648 | tf_op jit(solution)/shard_map/all_gather | solution.py:95
  7.9 86.2 %all-gather.3.cloned.1.call-start = ((), (), s32[]{:S(2)}) async-start(), calls=%async_computation.2 | async-start | bytes 1179648 | tf_op jit(solution)/shard_map/all_gather | solution.py:94
  8.7 222.4 %reduce-scatter.2.cloned.1.call-start = ((), (), s32[]{:S(2)}) async-start(), calls=%async_computation.4 | async-start | bytes 4587520 | tf_op jit(solution)/shard_map/reduce_scatter | solution.py:138
  184.7 0.7 copy-start.3
  184.7 0.9 copy-start
  184.7 1.0 copy-start.1
  184.7 12.0 %copy-start.4 = (s32[8]{0:T(128)S(1)}, s32[8]{0:T(128)}, u32[]{:S(2)}) copy-start(s32[8]{0:T(128)} %param.17) | copy-start | bytes 100
  191.2 17.3 %all-to-all-start = ((bf16[64,16,256]{2,1,0:T(8,128)(2,1)}), bf16[64,16,256]{2,1,0:T(8,128)(2,1)S(1)}, u32[]{:S(2)}, u32[]{:S(2)}) async-start(bf16[64,16,256]{2,1,0:T(8,128)(2,1)} %scatter_fusion), calls=%async_computation.1 | async-start | bytes 1048576 | tf_op jit(solution)/shard_map/all_to_all | solution.py:115
Sparse Core Ops, SparseCore 0:
  10.1 42.8 all-gather.4
  55.1 38.9 all-gather.2
  184.9 39.9 reduce-scatter.1
where the time goes:
time: 239 us; the launch traced here: 238 us
  waiting for transfers between devices  90.4 us (38%)
  matrix products  49.7 us (21%)
  other arithmetic  32.7 us (14%)
  local copies, waits for them, and re-layouts  31.7 us (13%)
  loops' own time  15.6 us (7%)
  between operations  13.9 us (6%)
  starting transfers between devices  3.61 us (2%)
    all_gather x1, waiting for transfers between devices, shards(): lax.all_gather(value_states, 'ctx', axis=0, tiled=True)  41.5 us
    all_gather x1, waiting for transfers between devices, shards(): lax.all_gather(key_states, 'ctx', axis=0, tiled=True)  38.8 us
    dot_general x8, matrix products, tile_update(): jnp.einsum('hgqk,khd->qhgd', weights.astype(jnp.bfloat16), value_tile, pr...  23.5 us
    dot_general x8, matrix products, tile_update(): jnp.einsum('qhgd,khd->hgqk', query_heads, key_tile, preferred_element_typ...  18 us
    another operation x1, loops' own time, attend_piece(): lax.scan(one_tile, soft_state, (key_blocks, value_blocks, jnp.arange(tile...  15.1 us
    reduce_sum x8, other arithmetic, tile_update(): norm_sum = norm_sum * factor + jnp.sum(weights, axis=-1)  12.1 us
    all_to_all x1, waiting for transfers between devices, shards(): lax.all_to_all(outgoing, 'ctx', split_axis=0, concat_axis=0, tiled=True)  8.75 us
    dot_general x1, matrix products, shards(): jnp.dot(attended, out_weight, preferred_element_type=jnp.float32)  8.28 us
  transfers between devices with their start and end apart: 4, of which 3 were waited for; matrix products, arithmetic and copies ran while one was open for 16% of the time, Pallas kernels for 0%

commit v1 on v0

v1 whole, which is shorter than its diff:
```python
import functools
import math

import jax
import jax.numpy as jnp
from jax import lax
from jax.experimental import pallas as pl
from jax.experimental.pallas import tpu as pltpu
from jax.sharding import PartitionSpec as P

HD = 128
PAGE = 16
BLOCK = 256
BLOCK_PAGES = BLOCK // PAGE
COLS = 512
SUM_ROWS = 16
FAR = 1e30
EXP2_SCALE = math.log2(math.e) / math.sqrt(HD)
MESH = pl.DeviceIdType.MESH


def ring_place(index, n):
    odd = lax.rem(index, 2)
    half = lax.div(index, 2)
    return half * (1 - odd) + (n - 1 - half) * odd


def ring_index(place, n):
    place = lax.rem(place + 4 * n, n)
    back = lax.div(place, n // 2)
    return 2 * place * (1 - back) + (2 * (n - 1 - place) + 1) * back


def dot(a, b, dims):
    return lax.dot_general(a, b, (dims, ((), ())), preferred_element_type=jnp.float32)


def kernel(
    n, heads, q_hbm, k_hbm, v_hbm, w_hbm, order_ref, owner_ref, held_ref,
    out_hbm, values_hbm, scales_hbm,
    kv, q, w, top, acc, att, own, core_out, core_in, y_out, y_in, result,
    table, table_s, store, store_out, scale_out,
    in_sems, ring_send, ring_recv, core_send, core_recv, y_send, y_recv, table_sem, out_sems,
):
    me = lax.axis_index("ctx")
    head = lax.axis_index("head")
    core = lax.rem(head, 2)
    y = lax.div(head, 2)
    place = ring_place(me, n)
    right = ring_index(place + 1, n)
    left = ring_index(place - 1, n)
    core_peer = head + 1 - 2 * core
    y_peer = lax.rem(head + 2, 4)
    d_model = w.shape[1]
    steps = d_model // COLS
    half = BLOCK // 2

    own_pages = pl.ds(me * 2 * BLOCK_PAGES, 2 * BLOCK_PAGES)
    loads = [
        pltpu.make_async_copy(k_hbm, kv.at[own_pages, :, pl.ds(0, HD)], in_sems.at[0]),
        pltpu.make_async_copy(v_hbm, kv.at[own_pages, :, pl.ds(HD, HD)], in_sems.at[1]),
        pltpu.make_async_copy(q_hbm, q, in_sems.at[2]),
        pltpu.make_async_copy(w_hbm, w, in_sems.at[3]),
    ]
    for load in loads:
        load.start()

    barrier = pltpu.get_barrier_semaphore()
    for peer in ((left, head), (right, head), (me, core_peer), (me, y_peer)):
        pl.semaphore_signal(barrier, inc=1, device_id=peer, device_id_type=MESH)
    pl.semaphore_wait(barrier, 4)
    loads[0].wait()
    loads[1].wait()

    def block_of(lane, number):
        if lane == 0:
            return ring_index(place - lax.div(number, 2), n) * 2 + lax.rem(number, 2)
        return ring_index(place + lax.div(number, 2), n) * 2 + 1 - lax.rem(number, 2)

    def got_block(lane, number):
        if lane == 0:
            return ring_index(place - 1 - lax.div(number, 2), n) * 2 + lax.rem(number, 2)
        return ring_index(place + 1 + lax.div(number, 2), n) * 2 + 1 - lax.rem(number, 2)

    def block_rows(block):
        return pl.ds(pl.multiple_of(block * BLOCK, BLOCK), BLOCK)

    def keys_of(block):
        return kv[pl.ds(block * BLOCK_PAGES, BLOCK_PAGES), :, 0:HD].reshape(BLOCK, HD)

    def values_of(block):
        return kv[pl.ds(block * BLOCK_PAGES, BLOCK_PAGES), :, HD : 2 * HD].reshape(BLOCK, HD)

    def hop(lane, number, block):
        rows = pl.ds(block * BLOCK_PAGES, BLOCK_PAGES)
        return pltpu.make_async_remote_copy(
            src_ref=kv.at[rows],
            dst_ref=kv.at[rows],
            send_sem=ring_send.at[lane, number],
            recv_sem=ring_recv.at[lane, number],
            device_id=(right if lane == 0 else left, head),
            device_id_type=MESH,
        )

    for number in range(2):
        for lane in range(2):
            hop(lane, jnp.int32(number), block_of(lane, jnp.int32(number))).start()
    loads[2].wait()

    def penalty(key_block, query_block):
        return jnp.where(order_ref[key_block] < order_ref[query_block], 0.0, FAR)

    def with_sums(block_a, block_b):
        vals = jnp.concatenate(
            [values_of(block_a).T, values_of(block_b).T], axis=1
        )
        return jnp.concatenate([vals, jnp.ones((SUM_ROWS, 2 * BLOCK), jnp.bfloat16)], axis=0)

    def local_step(part):
        mine = me * 2 + part
        other = me * 2 + 1 - part
        pen = penalty(other, mine)
        key_a = keys_of(mine)
        key_b = keys_of(other)
        vals = with_sums(mine, other)
        causal = lax.broadcasted_iota(jnp.int32, (BLOCK, BLOCK), 0) <= lax.broadcasted_iota(
            jnp.int32, (BLOCK, BLOCK), 1
        )
        for g in range(heads):
            query = q[block_rows(part), g * HD : (g + 1) * HD]
            s_a = jnp.where(causal, dot(key_a, query, ((1,), (1,))), -FAR)
            s_b = dot(key_b, query, ((1,), (1,)))
            new_top = jnp.maximum(
                jnp.max(s_a, axis=0, keepdims=True), jnp.max(s_b, axis=0, keepdims=True) - pen
            )
            base = new_top * EXP2_SCALE
            p_a = jnp.exp2(s_a * EXP2_SCALE - base).astype(jnp.bfloat16)
            p_b = jnp.exp2(s_b * EXP2_SCALE - (base + pen)).astype(jnp.bfloat16)
            top[g : g + 1, :] = new_top
            acc[g] = dot(vals, jnp.concatenate([p_a, p_b], axis=0), ((1,), (0,)))

    def pair_step(part, number):
        mine = me * 2 + part
        block_a = got_block(0, number)
        block_b = got_block(1, number)
        pen_a = penalty(block_a, mine)
        pen_b = penalty(block_b, mine)
        key_a = keys_of(block_a)
        key_b = keys_of(block_b)
        vals = with_sums(block_a, block_b)
        for g in range(heads):
            query = q[block_rows(part), g * HD : (g + 1) * HD]
            s_a = dot(key_a, query, ((1,), (1,)))
            s_b = dot(key_b, query, ((1,), (1,)))
            old_top = top[g : g + 1, :]
            new_top = jnp.maximum(
                old_top,
                jnp.maximum(
                    jnp.max(s_a, axis=0, keepdims=True) - pen_a,
                    jnp.max(s_b, axis=0, keepdims=True) - pen_b,
                ),
            )
            base = new_top * EXP2_SCALE
            p_a = jnp.exp2(s_a * EXP2_SCALE - (base + pen_a)).astype(jnp.bfloat16)
            p_b = jnp.exp2(s_b * EXP2_SCALE - (base + pen_b)).astype(jnp.bfloat16)
            factor = jnp.exp2(old_top * EXP2_SCALE - base)
            top[g : g + 1, :] = new_top
            acc[g] = acc[g] * factor + dot(
                vals, jnp.concatenate([p_a, p_b], axis=0), ((1,), (0,))
            )

    def finish():
        for g in range(heads):
            done = acc[g]
            scaled = done[0:HD] * (1.0 / done[HD : HD + 1])
            att[:, g * HD : (g + 1) * HD] = scaled.T.astype(jnp.bfloat16)

    def core_copy(turn, step):
        cols = pl.ds(step * COLS, COLS)
        return pltpu.make_async_remote_copy(
            src_ref=core_out.at[turn, :, cols],
            dst_ref=core_in.at[turn, :, cols],
            send_sem=core_send.at[turn, step],
            recv_sem=core_recv.at[turn, step],
            device_id=(me, core_peer),
            device_id_type=MESH,
        )

    def y_copy(step):
        cols = pl.ds(step * COLS, COLS)
        return pltpu.make_async_remote_copy(
            src_ref=y_out.at[:, cols],
            dst_ref=y_in.at[:, cols],
            send_sem=y_send.at[step],
            recv_sem=y_recv.at[step],
            device_id=(me, y_peer),
            device_id_type=MESH,
        )

    def project(turn, use):
        rows = att[...]
        for step in range(steps + 1):
            if step < steps:
                cols = slice(step * COLS, (step + 1) * COLS)
                sums = dot(rows, w[:, cols], ((1,), (0,)))
                first, second = sums[0:half], sums[half:BLOCK]
                keep_first = core == 0
                own[:, cols] = jnp.where(keep_first, first, second)
                core_out[turn, :, cols] = jnp.where(keep_first, second, first).astype(jnp.bfloat16)
                core_copy(turn, step).start()
            if step > 0:
                last = step - 1
                cols = slice(last * COLS, (last + 1) * COLS)
                core_copy(turn, last).wait_recv()
                use(last, own[:, cols] + core_in[turn, :, cols].astype(jnp.float32), cols)

    local_step(1 - y)

    @pl.loop(0, n - 1)
    def _(number):
        for lane in range(2):
            hop(lane, number, got_block(lane, number)).wait_recv()

        @pl.when(number < n - 3)
        def _():
            for lane in range(2):
                hop(lane, number + 2, got_block(lane, number)).start()

        pair_step(1 - y, number)

    finish()
    loads[3].wait()

    def send_y(step, sums, cols):
        y_out[:, cols] = sums.astype(jnp.bfloat16)
        y_copy(step).start()

    project(0, send_y)

    local_step(y)

    @pl.loop(0, n - 1)
    def _(number):
        pair_step(y, number)

    finish()

    def hold(step, sums, cols):
        own[:, cols] = sums

    project(1, hold)

    pages = owner_ref.shape[0]
    slots = store.shape[0] // PAGE
    mine = (owner_ref[...] == me).astype(jnp.int32)
    page_row = lax.broadcasted_iota(jnp.int32, (pages, pages), 0)
    page_col = lax.broadcasted_iota(jnp.int32, (pages, pages), 1)
    mine_col = jnp.sum(jnp.where(page_row == page_col, mine, 0), axis=0, keepdims=True)
    rank_col = jnp.sum(jnp.where(page_row < page_col, mine, 0), axis=0, keepdims=True)
    slot_col = jnp.where(mine_col > 0, held_ref[me] + rank_col, -1)
    slot_row = jnp.broadcast_to(slot_col, (slots, pages)).T
    slot_number = lax.broadcasted_iota(jnp.int32, (pages, slots), 1)
    page_number = lax.broadcasted_iota(jnp.int32, (pages, slots), 0)
    table[...] = jnp.broadcast_to(
        jnp.sum(jnp.where(slot_row == slot_number, page_number + 1, 0), axis=0, keepdims=True),
        table.shape,
    )
    to_scalars = pltpu.make_async_copy(table, table_s, table_sem)
    to_scalars.start()
    to_scalars.wait()

    @pl.loop(0, slots)
    def _(slot):
        entry = table_s[0, slot]
        held = jnp.where(entry > 0, 1.0, 0.0)
        page = kv[jnp.maximum(entry - 1, 0)].astype(jnp.float32) * held
        store[pl.ds(pl.multiple_of(slot * PAGE, PAGE), PAGE), :] = page

    @pl.loop(0, slots * PAGE // HD)
    def _(group):
        rows = pl.ds(pl.multiple_of(group * HD, HD), HD)
        for t in range(2):
            entries = store[rows, t * HD : (t + 1) * HD]
            size = jnp.abs(entries)
            scale = jnp.max(size, axis=1, keepdims=True) + 1e-06
            store_out[rows, t * HD : (t + 1) * HD] = (entries / scale).astype(jnp.bfloat16)
            scale_out[t : t + 1, rows] = jnp.max(size.T, axis=0, keepdims=True) + 1e-06

    page_copies = [
        pltpu.make_async_copy(store_out, values_hbm, out_sems.at[0]),
        pltpu.make_async_copy(scale_out, scales_hbm, out_sems.at[1]),
    ]
    for copy in page_copies:
        copy.start()

    out_copies = []
    for step in range(steps):
        cols = slice(step * COLS, (step + 1) * COLS)
        y_copy(step).wait_recv()
        result[:, cols] = (own[:, cols] + y_in[:, cols].astype(jnp.float32)).astype(jnp.bfloat16)
        span = pl.ds(step * COLS, COLS)
        copy = pltpu.make_async_copy(result.at[:, span], out_hbm.at[:, span], out_sems.at[2 + step])
        copy.start()
        out_copies.append(copy)

    @pl.loop(0, n - 1)
    def _(number):
        for lane in range(2):
            hop(lane, number, block_of(lane, number)).wait_send()

    for step in range(steps):
        core_copy(0, step).wait_send()
        core_copy(1, step).wait_send()
        y_copy(step).wait_send()
    for copy in page_copies + out_copies:
        copy.wait()


def shards(query_states, key_states, value_states, out_weight, block_order, page_owner, held_pages):
    n = lax.axis_size("ctx")
    tok_rows, col_count = query_states.shape
    d_model = out_weight.shape[1]
    heads = col_count // HD
    tokens = n * tok_rows
    pages_dev = tok_rows // PAGE
    slots = 2 * n * max(2, 2 * pages_dev // n)
    steps = d_model // COLS
    part = tok_rows // 4
    bf16, f32 = jnp.bfloat16, jnp.float32
    any_space = pl.BlockSpec(memory_space=pl.ANY)
    smem = pl.BlockSpec(memory_space=pltpu.SMEM)
    vmem = pl.BlockSpec(memory_space=pltpu.VMEM)
    layer_output, values, scales = pl.pallas_call(
        functools.partial(kernel, n, heads),
        out_shape=(
            jax.ShapeDtypeStruct((part, d_model), bf16),
            jax.ShapeDtypeStruct((slots * PAGE, 2 * HD), bf16),
            jax.ShapeDtypeStruct((2, slots * PAGE), f32),
        ),
        in_specs=[any_space] * 4 + [smem, vmem, smem],
        out_specs=(any_space,) * 3,
        scratch_shapes=[
            pltpu.VMEM((tokens // PAGE, PAGE, 2 * HD), bf16),
            pltpu.VMEM((tok_rows, col_count), bf16),
            pltpu.VMEM(out_weight.shape, bf16),
            pltpu.VMEM((8, BLOCK), f32),
            pltpu.VMEM((heads, HD + SUM_ROWS, BLOCK), f32),
            pltpu.VMEM((BLOCK, col_count), bf16),
            pltpu.VMEM((part, d_model), f32),
            pltpu.VMEM((2, part, d_model), bf16),
            pltpu.VMEM((2, part, d_model), bf16),
            pltpu.VMEM((part, d_model), bf16),
            pltpu.VMEM((part, d_model), bf16),
            pltpu.VMEM((part, d_model), bf16),
            pltpu.VMEM((8, slots), jnp.int32),
            pltpu.SMEM((8, slots), jnp.int32),
            pltpu.VMEM((slots * PAGE, 2 * HD), f32),
            pltpu.VMEM((slots * PAGE, 2 * HD), bf16),
            pltpu.VMEM((2, slots * PAGE), f32),
            pltpu.SemaphoreType.DMA((4,)),
            pltpu.SemaphoreType.DMA((2, n - 1)),
            pltpu.SemaphoreType.DMA((2, n - 1)),
            pltpu.SemaphoreType.DMA((2, steps)),
            pltpu.SemaphoreType.DMA((2, steps)),
            pltpu.SemaphoreType.DMA((steps,)),
            pltpu.SemaphoreType.DMA((steps,)),
            pltpu.SemaphoreType.DMA,
            pltpu.SemaphoreType.DMA((2 + steps,)),
        ],
        compiler_params=pltpu.CompilerParams(
            collective_id=0, has_side_effects=True, vmem_limit_bytes=48 * 1024 * 1024
        ),
    )(
        query_states,
        key_states.reshape(-1, PAGE, HD),
        value_states.reshape(-1, PAGE, HD),
        out_weight,
        block_order,
        page_owner,
        held_pages,
    )
    return layer_output, values.reshape(slots, PAGE, 2 * HD), scales


def solution(mesh):
    in_specs = (
        P("ctx", "head"),
        P("ctx", "head"),
        P("ctx", "head"),
        P("head", None),
        P(),
        P(),
        P(),
    )
    out_specs = (P(("ctx", "head"), None), P("ctx", None, "head"), P("head", "ctx"))
    return jax.shard_map(shards, mesh=mesh, in_specs=in_specs, out_specs=out_specs, check_vma=False)
```

time: 239 us -> 77.7 us (0.33)
  waiting for transfers between devices: 90.4 us -> 0 us
  Pallas kernels: 0 us -> 69.2 us
  matrix products: 49.7 us -> 0 us
  other arithmetic: 32.7 us -> 0 us
  local copies, waits for them, and re-layouts: 31.7 us -> 7.6 us
  loops' own time: 15.6 us -> 0 us
  between operations: 13.9 us -> 0.66 us
  starting transfers between devices: 3.61 us -> 0 us
    all_gather x2 -> x0, waiting for transfers between devices: 80.3 us -> none  [the longest x1 41.5 us: shards(): lax.all_gather(value_states, 'ctx', axis=0, tiled=True)]
    pallas_call x0 -> x1, Pallas kernels: none -> 69.2 us  [shards(): pl.pallas_call(functools.partial(kernel, n, heads), out_shape=(jax.ShapeD...]
    dot_general x17 -> x0, matrix products: 49.7 us -> none  [the longest x8 23.5 us: tile_update(): jnp.einsum('hgqk,khd->qhgd', weights.astype(jnp.bfloat16), value_tile, pr...]
    another operation x9 -> x0, loops' own time: 15.6 us -> none  [the longest x1 15.1 us: attend_piece(): lax.scan(one_tile, soft_state, (key_blocks, value_blocks, jnp.arange(tile...]
    reduce_sum x18 -> x0, other arithmetic: 13.1 us -> none  [the longest x8 12.1 us: tile_update(): norm_sum = norm_sum * factor + jnp.sum(weights, axis=-1)]
    all_to_all x1 -> x0, waiting for transfers between devices: 8.75 us -> none  [shards(): lax.all_to_all(outgoing, 'ctx', split_axis=0, concat_axis=0, tiled=True)]
    scatter x3 -> x0, local copies, waits for them, and re-layouts: 8 us -> none  [the longest x1 3.88 us: shards(): outgoing = jnp.zeros((ctx_count * per_peer, PAGE, row_width), jnp.bfloat1...]
    div x2 -> x0, local copies, waits for them, and re-layouts: 7.34 us -> none  [shards(): split_store / page_scale[..., None]]
  transfers between devices with their start and end apart: 4 -> 0, of which waited for: 3 -> 0; matrix products, arithmetic and copies ran while one was open for 16% -> 0% of each run, Pallas kernels for 0% -> 0%
where the time goes in v1:
time: 77.7 us; the launch traced here: 77.4 us
  Pallas kernels  69.2 us (89%)
  local copies, waits for them, and re-layouts  7.6 us (10%)
    pallas_call x1, Pallas kernels, shards(): pl.pallas_call(functools.partial(kernel, n, heads), out_shape=(jax.ShapeD...  69.2 us
    unnamed x14, local copies, waits for them, and re-layouts  7.6 us

profile of v1, /device:TPU:0, one launch (start us, length us, event | category | flops | bytes accessed | tf_op | source)
XLA Modules:
  0.0 77.4 jit_solution(4470597806232047195)
XLA Ops:
  0.6 0.8 %copy.10.owner_ref = s32[256,1]{1,0:T(8,128)S(1)} copy(s32[256,1]{0,1:T(1,128)} %param.12) | data formatting | bytes 2048 | tf_op args[5]
  1.4 0.0 copy-start
  1.5 1.2 %copy-done = bf16[512,896]{1,0:T(8,128)(2,1)S(1)} copy-done((bf16[512,896]{1,0:T(8,128)(2,1)S(1)}, bf16[512,896]{1,0:T(8,128)(2,1)}, u32[]{:S(2)}) %copy-start) | copy-done | bytes 917528
  2.6 0.0 copy-start.1
  2.6 0.9 %copy-done.1 = bf16[512,128]{1,0:T(8,128)(2,1)S(1)} copy-done((bf16[512,128]{1,0:T(8,128)(2,1)S(1)}, bf16[512,128]{1,0:T(8,128)(2,1)}, u32[]{:S(2)}) %copy-start.1) | copy-done | bytes 131096
  3.5 0.0 copy-start.2
  3.5 0.9 %copy-done.2 = bf16[512,128]{1,0:T(8,128)(2,1)S(1)} copy-done((bf16[512,128]{1,0:T(8,128)(2,1)S(1)}, bf16[512,128]{1,0:T(8,128)(2,1)}, u32[]{:S(2)}) %copy-start.2) | copy-done | bytes 131096
  4.4 0.0 copy-start.3
  4.4 0.7 copy-done.3
  5.1 0.0 copy-start.4
  5.1 0.7 copy-done.4
  5.8 69.2 %shard_map.94 = (bf16[128,3584]{1,0:T(8,128)(2,1)S(1)}, bf16[2048,256]{1,0:T(8,128)(2,1)S(1)}, f32[2,2048]{1,0:T(2,128)S(1)}) custom-call(bf16[512,896]{1,0:T(8,128)(2,1)S(1)} %copy-done, bf16[32,16,128]{2,1,0:T(8,128)(2,1)S(1)} %bitcast.4, bf16[32,16,128]{2,1,0:T(8,128)(2,1)S(1)} %bitcast.5, bf16[896,3584]{1,0:T(8,128)(2,1)} %w_hbm.1, s32[16]{0:T(128)S(1)} %copy-done.3, ...), custom_call_target="tpu_custom_call" | custom-call | tf_op jit(solution)/shard_map/pallas_call | solution.py:333
  74.9 0.9 %copy.14 = bf16[128,3584]{1,0:T(8,128)(2,1)} copy(bf16[128,3584]{1,0:T(8,128)(2,1)S(1)} %get-tuple-element.12) | data formatting | bytes 1835008
  75.9 1.0 %copy.15 = bf16[128,16,256]{2,1,0:T(8,128)(2,1)} copy(bf16[128,16,256]{2,1,0:T(8,128)(2,1)S(1)} %bitcast.3) | data formatting | bytes 2097152
  76.8 0.6 copy.16
Async XLA Ops:
  1.4 1.2 %copy-start = (bf16[512,896]{1,0:T(8,128)(2,1)S(1)}, bf16[512,896]{1,0:T(8,128)(2,1)}, u32[]{:S(2)}) copy-start(bf16[512,896]{1,0:T(8,128)(2,1)} %q_hbm.1) | copy-start | bytes 2752516
  2.6 0.9 %copy-start.1 = (bf16[512,128]{1,0:T(8,128)(2,1)S(1)}, bf16[512,128]{1,0:T(8,128)(2,1)}, u32[]{:S(2)}) copy-start(bf16[512,128]{1,0:T(8,128)(2,1)} %param.8) | copy-start | bytes 393220
  3.5 0.9 %copy-start.2 = (bf16[512,128]{1,0:T(8,128)(2,1)S(1)}, bf16[512,128]{1,0:T(8,128)(2,1)}, u32[]{:S(2)}) copy-start(bf16[512,128]{1,0:T(8,128)(2,1)} %param.9) | copy-start | bytes 393220
  4.4 0.7 copy-start.3
  5.1 0.7 copy-start.4

commit v2 on v1

--- a/solution.py
+++ b/solution.py
@@ -38,7 +38,7 @@
 def kernel(
     n, heads, q_hbm, k_hbm, v_hbm, w_hbm, order_ref, owner_ref, held_ref,
     out_hbm, values_hbm, scales_hbm,
-    kv, q, w, top, acc, att, own, core_out, core_in, y_out, y_in, result,
+    kv, q, q_t, w, top, acc, att, own, core_out, core_in, y_out, y_in, result,
     table, table_s, store, store_out, scale_out,
     in_sems, ring_send, ring_recv, core_send, core_recv, y_send, y_recv, table_sem, out_sems,
 ):
@@ -106,6 +106,10 @@
         for lane in range(2):
             hop(lane, jnp.int32(number), block_of(lane, jnp.int32(number))).start()
     loads[2].wait()
+    for g in range(heads):
+        for part in range(2):
+            rows = slice(part * BLOCK, (part + 1) * BLOCK)
+            q_t[part, g] = q[rows, g * HD : (g + 1) * HD].T
 
     def penalty(key_block, query_block):
         return jnp.where(order_ref[key_block] < order_ref[query_block], 0.0, FAR)
@@ -116,7 +120,7 @@
         )
         return jnp.concatenate([vals, jnp.ones((SUM_ROWS, 2 * BLOCK), jnp.bfloat16)], axis=0)
 
-    def local_step(part):
+    def local_step(slot, part):
         mine = me * 2 + part
         other = me * 2 + 1 - part
         pen = penalty(other, mine)
@@ -127,19 +131,19 @@
             jnp.int32, (BLOCK, BLOCK), 1
         )
         for g in range(heads):
-            query = q[block_rows(part), g * HD : (g + 1) * HD]
-            s_a = jnp.where(causal, dot(key_a, query, ((1,), (1,))), -FAR)
-            s_b = dot(key_b, query, ((1,), (1,)))
+            query = q_t[part, g]
+            s_a = jnp.where(causal, dot(key_a, query, ((1,), (0,))), -FAR)
+            s_b = dot(key_b, query, ((1,), (0,)))
             new_top = jnp.maximum(
                 jnp.max(s_a, axis=0, keepdims=True), jnp.max(s_b, axis=0, keepdims=True) - pen
             )
             base = new_top * EXP2_SCALE
             p_a = jnp.exp2(s_a * EXP2_SCALE - base).astype(jnp.bfloat16)
             p_b = jnp.exp2(s_b * EXP2_SCALE - (base + pen)).astype(jnp.bfloat16)
-            top[g : g + 1, :] = new_top
-            acc[g] = dot(vals, jnp.concatenate([p_a, p_b], axis=0), ((1,), (0,)))
-
-    def pair_step(part, number):
+            top[slot, g : g + 1, :] = new_top
+            acc[slot, g] = dot(vals, jnp.concatenate([p_a, p_b], axis=0), ((1,), (0,)))
+
+    def pair_step(slot, part, number):
         mine = me * 2 + part
         block_a = got_block(0, number)
         block_b = got_block(1, number)
@@ -149,10 +153,10 @@
         key_b = keys_of(block_b)
         vals = with_sums(block_a, block_b)
         for g in range(heads):
-            query = q[block_rows(part), g * HD : (g + 1) * HD]
-            s_a = dot(key_a, query, ((1,), (1,)))
-            s_b = dot(key_b, query, ((1,), (1,)))
-            old_top = top[g : g + 1, :]
+            query = q_t[part, g]
+            s_a = dot(key_a, query, ((1,), (0,)))
+            s_b = dot(key_b, query, ((1,), (0,)))
+            old_top = top[slot, g : g + 1, :]
             new_top = jnp.maximum(
                 old_top,
                 jnp.maximum(
@@ -164,14 +168,14 @@
             p_a = jnp.exp2(s_a * EXP2_SCALE - (base + pen_a)).astype(jnp.bfloat16)
             p_b = jnp.exp2(s_b * EXP2_SCALE - (base + pen_b)).astype(jnp.bfloat16)
             factor = jnp.exp2(old_top * EXP2_SCALE - base)
-            top[g : g + 1, :] = new_top
-            acc[g] = acc[g] * factor + dot(
+            top[slot, g : g + 1, :] = new_top
+            acc[slot, g] = acc[slot, g] * factor + dot(
                 vals, jnp.concatenate([p_a, p_b], axis=0), ((1,), (0,))
             )
 
-    def finish():
+    def finish(slot):
         for g in range(heads):
-            done = acc[g]
+            done = acc[slot, g]
             scaled = done[0:HD] * (1.0 / done[HD : HD + 1])
             att[:, g * HD : (g + 1) * HD] = scaled.T.astype(jnp.bfloat16)
 
@@ -197,24 +201,24 @@
             device_id_type=MESH,
         )
 
-    def project(turn, use):
+    def project(turn):
         rows = att[...]
-        for step in range(steps + 1):
-            if step < steps:
-                cols = slice(step * COLS, (step + 1) * COLS)
-                sums = dot(rows, w[:, cols], ((1,), (0,)))
-                first, second = sums[0:half], sums[half:BLOCK]
-                keep_first = core == 0
-                own[:, cols] = jnp.where(keep_first, first, second)
-                core_out[turn, :, cols] = jnp.where(keep_first, second, first).astype(jnp.bfloat16)
-                core_copy(turn, step).start()
-            if step > 0:
-                last = step - 1
-                cols = slice(last * COLS, (last + 1) * COLS)
-                core_copy(turn, last).wait_recv()
-                use(last, own[:, cols] + core_in[turn, :, cols].astype(jnp.float32), cols)
-
-    local_step(1 - y)
+        for step in range(steps):
+            cols = slice(step * COLS, (step + 1) * COLS)
+            sums = dot(rows, w[:, cols], ((1,), (0,)))
+            first, second = sums[0:half], sums[half:BLOCK]
+            keep_first = core == 0
+            own[:, cols] = jnp.where(keep_first, first, second)
+            core_out[turn, :, cols] = jnp.where(keep_first, second, first).astype(jnp.bfloat16)
+            core_copy(turn, step).start()
+
+    def both_cores(turn, step):
+        cols = slice(step * COLS, (step + 1) * COLS)
+        core_copy(turn, step).wait_recv()
+        return own[:, cols] + core_in[turn, :, cols].astype(jnp.float32), cols
+
+    local_step(0, 1 - y)
+    local_step(1, y)
 
     @pl.loop(0, n - 1)
     def _(number):
@@ -226,36 +230,31 @@
             for lane in range(2):
                 hop(lane, number + 2, got_block(lane, number)).start()
 
-        pair_step(1 - y, number)
-
-    finish()
+        pair_step(0, 1 - y, number)
+
+    finish(0)
     loads[3].wait()
 
-    def send_y(step, sums, cols):
+    project(0)
+    for step in range(steps):
+        sums, cols = both_cores(0, step)
         y_out[:, cols] = sums.astype(jnp.bfloat16)
         y_copy(step).start()
 
-    project(0, send_y)
-
-    local_step(y)
-
     @pl.loop(0, n - 1)
     def _(number):
-        pair_step(y, number)
-
-    finish()
-
-    def hold(step, sums, cols):
-        own[:, cols] = sums
-
-    project(1, hold)
-
-    pages = owner_ref.shape[0]
+        pair_step(1, y, number)
+
+    finish(1)
+
+    project(1)
+
+    pages = owner_ref.shape[1]
     slots = store.shape[0] // PAGE
-    mine = (owner_ref[...] == me).astype(jnp.int32)
+    mine_col = (owner_ref[...] == me).astype(jnp.int32)
+    mine = jnp.broadcast_to(mine_col, (slots, pages)).T[:, 0:1]
     page_row = lax.broadcasted_iota(jnp.int32, (pages, pages), 0)
     page_col = lax.broadcasted_iota(jnp.int32, (pages, pages), 1)
-    mine_col = jnp.sum(jnp.where(page_row == page_col, mine, 0), axis=0, keepdims=True)
     rank_col = jnp.sum(jnp.where(page_row < page_col, mine, 0), axis=0, keepdims=True)
     slot_col = jnp.where(mine_col > 0, held_ref[me] + rank_col, -1)
     slot_row = jnp.broadcast_to(slot_col, (slots, pages)).T
@@ -269,14 +268,14 @@
     to_scalars.start()
     to_scalars.wait()
 
-    @pl.loop(0, slots)
+    @pl.loop(0, slots, unroll=8)
     def _(slot):
         entry = table_s[0, slot]
         held = jnp.where(entry > 0, 1.0, 0.0)
         page = kv[jnp.maximum(entry - 1, 0)].astype(jnp.float32) * held
         store[pl.ds(pl.multiple_of(slot * PAGE, PAGE), PAGE), :] = page
 
-    @pl.loop(0, slots * PAGE // HD)
+    @pl.loop(0, slots * PAGE // HD, unroll=2)
     def _(group):
         rows = pl.ds(pl.multiple_of(group * HD, HD), HD)
         for t in range(2):
@@ -295,9 +294,9 @@
 
     out_copies = []
     for step in range(steps):
-        cols = slice(step * COLS, (step + 1) * COLS)
+        sums, cols = both_cores(1, step)
         y_copy(step).wait_recv()
-        result[:, cols] = (own[:, cols] + y_in[:, cols].astype(jnp.float32)).astype(jnp.bfloat16)
+        result[:, cols] = (sums + y_in[:, cols].astype(jnp.float32)).astype(jnp.bfloat16)
         span = pl.ds(step * COLS, COLS)
         copy = pltpu.make_async_copy(result.at[:, span], out_hbm.at[:, span], out_sems.at[2 + step])
         copy.start()
@@ -327,7 +326,7 @@
     steps = d_model // COLS
     part = tok_rows // 4
     bf16, f32 = jnp.bfloat16, jnp.float32
-    any_space = pl.BlockSpec(memory_space=pl.ANY)
+    hbm = pl.BlockSpec(memory_space=pltpu.HBM)
     smem = pl.BlockSpec(memory_space=pltpu.SMEM)
     vmem = pl.BlockSpec(memory_space=pltpu.VMEM)
     layer_output, values, scales = pl.pallas_call(
@@ -337,14 +336,15 @@
             jax.ShapeDtypeStruct((slots * PAGE, 2 * HD), bf16),
             jax.ShapeDtypeStruct((2, slots * PAGE), f32),
         ),
-        in_specs=[any_space] * 4 + [smem, vmem, smem],
-        out_specs=(any_space,) * 3,
+        in_specs=[hbm] * 4 + [smem, vmem, smem],
+        out_specs=(hbm,) * 3,
         scratch_shapes=[
             pltpu.VMEM((tokens // PAGE, PAGE, 2 * HD), bf16),
             pltpu.VMEM((tok_rows, col_count), bf16),
+            pltpu.VMEM((2, heads, HD, BLOCK), bf16),
             pltpu.VMEM(out_weight.shape, bf16),
-            pltpu.VMEM((8, BLOCK), f32),
-            pltpu.VMEM((heads, HD + SUM_ROWS, BLOCK), f32),
+            pltpu.VMEM((2, 8, BLOCK), f32),
+            pltpu.VMEM((2, heads, HD + SUM_ROWS, BLOCK), f32),
             pltpu.VMEM((BLOCK, col_count), bf16),
             pltpu.VMEM((part, d_model), f32),
             pltpu.VMEM((2, part, d_model), bf16),
@@ -368,7 +368,7 @@
             pltpu.SemaphoreType.DMA((2 + steps,)),
         ],
         compiler_params=pltpu.CompilerParams(
-            collective_id=0, has_side_effects=True, vmem_limit_bytes=48 * 1024 * 1024
+            collective_id=0, has_side_effects=True, vmem_limit_bytes=63 * 1024 * 1024
         ),
     )(
         query_states,
@@ -376,7 +376,7 @@
         value_states.reshape(-1, PAGE, HD),
         out_weight,
         block_order,
-        page_owner,
+        page_owner.reshape(1, -1),
         held_pages,
     )
     return layer_output, values.reshape(slots, PAGE, 2 * HD), scales

time: 77.7 us -> 66.3 us (0.85)
  Pallas kernels: 69.2 us -> 58.9 us
  local copies, waits for them, and re-layouts: 7.6 us -> 5.74 us
    pallas_call x1, Pallas kernels: 69.2 us -> 58.9 us  [shards(): pl.pallas_call(functools.partial(kernel, n, heads), out_shape=(jax.ShapeD...]
    unnamed x14 -> x3, local copies, waits for them, and re-layouts: 7.6 us -> 5.74 us
where the time goes in v2:
time: 66.3 us; the launch traced here: 65.3 us
  Pallas kernels  58.9 us (89%)
  local copies, waits for them, and re-layouts  5.74 us (9%)
    pallas_call x1, Pallas kernels, shards(): pl.pallas_call(functools.partial(kernel, n, heads), out_shape=(jax.ShapeD...  58.9 us
    unnamed x3, local copies, waits for them, and re-layouts  5.74 us

profile of v2, /device:TPU:0, one launch (start us, length us, event | category | flops | bytes accessed | tf_op | source)
XLA Modules:
  0.0 65.3 jit_solution(14463048208852697043)
XLA Ops:
  0.6 58.9 %shard_map.94 = (bf16[128,3584]{1,0:T(8,128)(2,1)}, bf16[2048,256]{1,0:T(8,128)(2,1)}, f32[2,2048]{1,0:T(2,128)}) custom-call(bf16[512,896]{1,0:T(8,128)(2,1)} %q_hbm.1, bf16[32,16,128]{2,1,0:T(8,128)(2,1)} %bitcast.5, bf16[32,16,128]{2,1,0:T(8,128)(2,1)} %bitcast.6, bf16[896,3584]{1,0:T(8,128)(2,1)} %w_hbm.1, s32[16]{0:T(128)} %order_ref.1, ...), custom_call_target="tpu_custom_call" | custom-call | tf_op jit(solution)/shard_map/pallas_call | solution.py:332
  59.6 2.2 %copy.13 = bf16[128,3584]{1,0:T(8,128)(2,1)} copy(bf16[128,3584]{1,0:T(8,128)(2,1)} %get-tuple-element.12) | data formatting | bytes 1835008
  61.7 2.3 %copy.14 = bf16[128,16,256]{2,1,0:T(8,128)(2,1)} copy(bf16[128,16,256]{2,1,0:T(8,128)(2,1)} %bitcast.4) | data formatting | bytes 2097152
  64.0 1.3 %copy.15 = f32[2,2048]{1,0:T(2,128)} copy(f32[2,2048]{1,0:T(2,128)} %get-tuple-element.14) | data formatting | bytes 32768

commit v3 on v2

--- a/solution.py
+++ b/solution.py
@@ -39,7 +39,7 @@
     n, heads, q_hbm, k_hbm, v_hbm, w_hbm, order_ref, owner_ref, held_ref,
     out_hbm, values_hbm, scales_hbm,
     kv, q, q_t, w, top, acc, att, own, core_out, core_in, y_out, y_in, result,
-    table, table_s, store, store_out, scale_out,
+    table, table_s, store_out, scale_out,
     in_sems, ring_send, ring_recv, core_send, core_recv, y_send, y_recv, table_sem, out_sems,
 ):
     me = lax.axis_index("ctx")
@@ -220,37 +220,8 @@
     local_step(0, 1 - y)
     local_step(1, y)
 
-    @pl.loop(0, n - 1)
-    def _(number):
-        for lane in range(2):
-            hop(lane, number, got_block(lane, number)).wait_recv()
-
-        @pl.when(number < n - 3)
-        def _():
-            for lane in range(2):
-                hop(lane, number + 2, got_block(lane, number)).start()
-
-        pair_step(0, 1 - y, number)
-
-    finish(0)
-    loads[3].wait()
-
-    project(0)
-    for step in range(steps):
-        sums, cols = both_cores(0, step)
-        y_out[:, cols] = sums.astype(jnp.bfloat16)
-        y_copy(step).start()
-
-    @pl.loop(0, n - 1)
-    def _(number):
-        pair_step(1, y, number)
-
-    finish(1)
-
-    project(1)
-
     pages = owner_ref.shape[1]
-    slots = store.shape[0] // PAGE
+    slots = table.shape[1]
     mine_col = (owner_ref[...] == me).astype(jnp.int32)
     mine = jnp.broadcast_to(mine_col, (slots, pages)).T[:, 0:1]
     page_row = lax.broadcasted_iota(jnp.int32, (pages, pages), 0)
@@ -268,22 +239,52 @@
     to_scalars.start()
     to_scalars.wait()
 
-    @pl.loop(0, slots, unroll=8)
-    def _(slot):
-        entry = table_s[0, slot]
-        held = jnp.where(entry > 0, 1.0, 0.0)
-        page = kv[jnp.maximum(entry - 1, 0)].astype(jnp.float32) * held
-        store[pl.ds(pl.multiple_of(slot * PAGE, PAGE), PAGE), :] = page
+    @pl.loop(0, n - 1)
+    def _(number):
+        for lane in range(2):
+            hop(lane, number, got_block(lane, number)).wait_recv()
+
+        @pl.when(number < n - 3)
+        def _():
+            for lane in range(2):
+                hop(lane, number + 2, got_block(lane, number)).start()
+
+        pair_step(0, 1 - y, number)
+
+    finish(0)
+    loads[3].wait()
+
+    project(0)
+    for step in range(steps):
+        sums, cols = both_cores(0, step)
+        y_out[:, cols] = sums.astype(jnp.bfloat16)
+        y_copy(step).start()
+
+    @pl.loop(0, n - 1)
+    def _(number):
+        pair_step(1, y, number)
+
+    finish(1)
+
+    project(1)
 
     @pl.loop(0, slots * PAGE // HD, unroll=2)
     def _(group):
         rows = pl.ds(pl.multiple_of(group * HD, HD), HD)
+        found = []
+        for number in range(HD // PAGE):
+            entry = table_s[0, group * (HD // PAGE) + number]
+            held = jnp.where(entry > 0, 1.0, 0.0)
+            found.append(kv[jnp.maximum(entry - 1, 0)].astype(jnp.float32) * held)
+        found = jnp.concatenate(found, axis=0)
+        same = lax.broadcasted_iota(jnp.int32, (HD, HD), 0) == lax.broadcasted_iota(
+            jnp.int32, (HD, HD), 1
+        )
         for t in range(2):
-            entries = store[rows, t * HD : (t + 1) * HD]
-            size = jnp.abs(entries)
-            scale = jnp.max(size, axis=1, keepdims=True) + 1e-06
+            entries = found[:, t * HD : (t + 1) * HD]
+            scale = jnp.max(jnp.abs(entries), axis=1, keepdims=True) + 1e-06
             store_out[rows, t * HD : (t + 1) * HD] = (entries / scale).astype(jnp.bfloat16)
-            scale_out[t : t + 1, rows] = jnp.max(size.T, axis=0, keepdims=True) + 1e-06
+            scale_out[t : t + 1, rows] = jnp.sum(jnp.where(same, scale, 0.0), axis=0, keepdims=True)
 
     page_copies = [
         pltpu.make_async_copy(store_out, values_hbm, out_sems.at[0]),
@@ -354,7 +355,6 @@
             pltpu.VMEM((part, d_model), bf16),
             pltpu.VMEM((8, slots), jnp.int32),
             pltpu.SMEM((8, slots), jnp.int32),
-            pltpu.VMEM((slots * PAGE, 2 * HD), f32),
             pltpu.VMEM((slots * PAGE, 2 * HD), bf16),
             pltpu.VMEM((2, slots * PAGE), f32),
             pltpu.SemaphoreType.DMA((4,)),

time: 66.3 us -> 64.8 us (0.977)
  Pallas kernels: 58.9 us -> 57.5 us
    pallas_call x1, Pallas kernels: 58.9 us -> 57.5 us  [shards(): pl.pallas_call(functools.partial(kernel, n, heads), out_shape=(jax.ShapeD...]
where the time goes in v3:
time: 64.8 us; the launch traced here: 63.8 us
  Pallas kernels  57.5 us (89%)
  local copies, waits for them, and re-layouts  5.74 us (9%)
    pallas_call x1, Pallas kernels, shards(): pl.pallas_call(functools.partial(kernel, n, heads), out_shape=(jax.ShapeD...  57.5 us
    unnamed x3, local copies, waits for them, and re-layouts  5.74 us

profile of v3, /device:TPU:0, one launch (start us, length us, event | category | flops | bytes accessed | tf_op | source)
XLA Modules:
  0.0 63.8 jit_solution(18048358048510825628)
XLA Ops:
  0.6 57.5 %shard_map.94 = (bf16[128,3584]{1,0:T(8,128)(2,1)}, bf16[2048,256]{1,0:T(8,128)(2,1)}, f32[2,2048]{1,0:T(2,128)}) custom-call(bf16[512,896]{1,0:T(8,128)(2,1)} %q_hbm.1, bf16[32,16,128]{2,1,0:T(8,128)(2,1)} %bitcast.5, bf16[32,16,128]{2,1,0:T(8,128)(2,1)} %bitcast.6, bf16[896,3584]{1,0:T(8,128)(2,1)} %w_hbm.1, s32[16]{0:T(128)} %order_ref.1, ...), custom_call_target="tpu_custom_call" | custom-call | tf_op jit(solution)/shard_map/pallas_call | solution.py:333
  58.1 2.2 %copy.13 = bf16[128,3584]{1,0:T(8,128)(2,1)} copy(bf16[128,3584]{1,0:T(8,128)(2,1)} %get-tuple-element.12) | data formatting | bytes 1835008
  60.3 2.3 %copy.14 = bf16[128,16,256]{2,1,0:T(8,128)(2,1)} copy(bf16[128,16,256]{2,1,0:T(8,128)(2,1)} %bitcast.4) | data formatting | bytes 2097152
  62.5 1.3 %copy.15 = f32[2,2048]{1,0:T(2,128)} copy(f32[2,2048]{1,0:T(2,128)} %get-tuple-element.14) | data formatting | bytes 32768
